TPU v7x, 256 devices: a whole 4x4x8 slice. The times are simulated.
256 devices in a mesh: gx: 32 (over y, z), gy: 8 (over x, core).
Axes of the slice: x: 4, y: 4, z: 8, core: 2. Of those that a mesh axis runs over, the one named last changes fastest.
Arguments:
- features: bfloat16 [32, 4, 256, 1024], P(None, None, 'gx', 'gy'), may hold values from -8 to 8
- vessel_label: int32 [4, 256, 1024], P(None, 'gx', 'gy'), may hold values from 0 to 1, as said below
- conv_weight: bfloat16 [27, 32], replicated, may hold values from -0.21875 to 0.21875
- conv_bias: float32 [1], replicated, may hold values from -1.5 to 1.5
Outputs:
- cldice_loss: float32 [], replicated
- weight_grad: float32 [27, 32], replicated
- bias_grad: float32 [1], replicated
- feature_grad: bfloat16 [32, 4, 256, 1024], P(None, None, 'gx', 'gy')
Inputs may be any that keep to these rules, and one draw needn't show every extreme that they name: `vessel_label`: 1 marks a vessel voxel, 0 the background.
All inputs are finite; a program needn't handle non-finite values.
Results may differ from a plain program's by a relative error of at most 0.012.
Values may be sent and summed in bfloat16 or wider, within the bound.
No kernel may reach another device: no remote copies, remote signals or barrier semaphores. Data moves between devices by JAX's collectives and lax.ppermute only.
A program may use at most 64 MiB of HBM per device.

v0:
```python
import jax
import jax.numpy as jnp
from jax import lax
from jax.sharding import PartitionSpec as P

ITERS = 5
softmin_sharpness = 0.1
softness = 0.05


def padded_2(x, sides, width):
    for axis, dim in sides:
        size, length = (lax.axis_size(axis), x.shape[dim])
        up = [(i, (i + 1) % size) for i in range(size - 1)]
        down = [(j, i) for i, j in up]
        last = lax.slice_in_dim(x, length - width, length, axis=dim)
        initial = lax.slice_in_dim(x, 0, width, axis=dim)
        before = lax.ppermute(last, axis, up)
        after = lax.ppermute(initial, axis, down)
        x = jnp.concatenate([before, x, after], axis=dim)
    return x


def passed_along(value, axis, steps):
    count = lax.axis_size(axis)
    initial, last = (max(0, -steps), min(count, count - steps))
    return lax.ppermute(value, axis, [(source, source + steps) for source in range(initial, last)])


def soft_relu(source_grid):
    return softness * jax.nn.softplus(source_grid / softness)


def crop_cycle(array, amount):
    if amount == 0:
        return array
    return array[..., amount : array.shape[-2] - amount, amount : array.shape[-1] - amount]


def border_thickness(source_grid):
    widths = [(0, 0)] * (source_grid.ndim - 3) + [(1, 1), (0, 0), (0, 0)]
    return jnp.pad(source_grid, widths)


def soft_dilate(source_grid, cell_neighbourhood):
    scaled_powers = jnp.exp(border_thickness(source_grid) / softmin_sharpness)
    collapsed_aggregate = scaled_powers[:-2] + scaled_powers[1:-1] + scaled_powers[2:]
    collapsed_aggregate = (
        collapsed_aggregate[:, :-2] + collapsed_aggregate[:, 1:-1] + collapsed_aggregate[:, 2:]
    )
    collapsed_aggregate = (
        collapsed_aggregate[:, :, :-2]
        + collapsed_aggregate[:, :, 1:-1]
        + collapsed_aggregate[:, :, 2:]
    )
    return softmin_sharpness * jnp.log(collapsed_aggregate / 27.0) * cell_neighbourhood


def soft_erode(source_grid, cell_neighbourhood):
    scaled_powers = jnp.exp(-border_thickness(source_grid) / softmin_sharpness)
    middle_cell = scaled_powers[1:-1, 1:-1, 1:-1]
    neighbouring_cells = (
        scaled_powers[2:, 1:-1, 1:-1]
        + scaled_powers[:-2, 1:-1, 1:-1]
        + scaled_powers[1:-1, 2:, 1:-1]
        + scaled_powers[1:-1, :-2, 1:-1]
        + scaled_powers[1:-1, 1:-1, 2:]
        + scaled_powers[1:-1, 1:-1, :-2]
    )
    return (
        -softmin_sharpness
        * jnp.log(middle_cell / 3.0 + neighbouring_cells / 9.0)
        * cell_neighbourhood
    )


def soft_open(source_grid, cell_neighbourhood):
    return soft_dilate(
        soft_erode(source_grid, crop_cycle(cell_neighbourhood, 1)),
        crop_cycle(cell_neighbourhood, 2),
    )


def skeleton(source_grid, cell_neighbourhood, cycle_width):
    current = source_grid
    mask_now = cell_neighbourhood
    opened = soft_open(crop_cycle(current, cycle_width - 2), crop_cycle(mask_now, cycle_width - 2))
    skeleton_sum = soft_relu(crop_cycle(current, cycle_width) - opened)
    for erosion in range(1, cycle_width - 1):
        mask_now = crop_cycle(mask_now, 1)
        current = soft_erode(current, mask_now)
        cycle_now = cycle_width - erosion
        opened = soft_open(crop_cycle(current, cycle_now - 2), crop_cycle(mask_now, cycle_now - 2))
        change_term = soft_relu(crop_cycle(current, cycle_now) - opened)
        skeleton_sum = skeleton_sum + soft_relu(change_term - skeleton_sum * change_term)
    return skeleton_sum


def topology_loss(totals):
    precision = (totals[0] + 1.0) / (totals[1] + 1.0)
    sensitivity = (totals[2] + 1.0) / (totals[3] + 1.0)
    return 1.0 - 2.0 * precision * sensitivity / (precision + sensitivity)


def inside_mask(cycle_width, tile_rows, tile_cols):
    row_start = lax.axis_index("gx") * tile_rows - cycle_width
    col_start = lax.axis_index("gy") * tile_cols - cycle_width
    row_ids = row_start + jnp.arange(tile_rows + 2 * cycle_width, dtype=jnp.int32)
    col_ids = col_start + jnp.arange(tile_cols + 2 * cycle_width, dtype=jnp.int32)
    row_inside = (row_ids >= 0) & (row_ids < tile_rows * lax.axis_size("gx"))
    col_inside = (col_ids >= 0) & (col_ids < tile_cols * lax.axis_size("gy"))
    return (row_inside[:, None] & col_inside[None, :]).astype(jnp.float32)


def intersection_sums(prob_cycle, label_cycle, label_skeleton, cell_neighbourhood, cycle_width):
    pred_skeleton = skeleton(prob_cycle, cell_neighbourhood, cycle_width)
    prob_own = crop_cycle(prob_cycle, cycle_width)
    label_own = crop_cycle(label_cycle, cycle_width)
    return (
        jnp.sum(pred_skeleton * label_own),
        jnp.sum(pred_skeleton),
        jnp.sum(label_skeleton * prob_own),
        jnp.sum(label_skeleton),
    )


def extend(block, halo_width):
    return padded_2(block, (("gx", 2), ("gy", 3)), halo_width)


def convolve(feature_cycle, conv_weight, conv_bias):
    padded = border_thickness(feature_cycle)
    products = jnp.einsum("kc,czxy->kzxy", conv_weight, padded, preferred_element_type=jnp.float32)
    depth_cells = feature_cycle.shape[1]
    out_rows = feature_cycle.shape[2] - 2
    out_cols = feature_cycle.shape[3] - 2
    logits = jnp.zeros((depth_cells, out_rows, out_cols), jnp.float32) + conv_bias[0]
    for position in range(27):
        depth_shift, row_shift, col_shift = (position // 9, position // 3 % 3, position % 3)
        logits = (
            logits
            + products[
                position,
                depth_shift : depth_shift + depth_cells,
                row_shift : row_shift + out_rows,
                col_shift : col_shift + out_cols,
            ]
        )
    return (padded, logits)


def shifted_stack(grad_logits):
    pieces = []
    for position in range(27):
        depth_shift, row_shift, col_shift = (position // 9, position // 3 % 3, position % 3)
        pieces.append(
            jnp.pad(
                grad_logits,
                (
                    (depth_shift, 2 - depth_shift),
                    (row_shift, 2 - row_shift),
                    (col_shift, 2 - col_shift),
                ),
            )
        )
    stacked = jnp.stack(pieces)
    upper_part = stacked.astype(jnp.bfloat16)
    lower_part = (stacked - upper_part.astype(jnp.float32)).astype(jnp.bfloat16)
    return (upper_part, lower_part)


def weight_terms(upper_part, lower_part, padded):
    first = jnp.einsum("kzxy,czxy->kc", upper_part, padded, preferred_element_type=jnp.float32)
    return first + jnp.einsum(
        "kzxy,czxy->kc", lower_part, padded, preferred_element_type=jnp.float32
    )


def feature_terms(upper_part, lower_part, conv_weight):
    first = jnp.einsum("kc,kzxy->czxy", conv_weight, upper_part, preferred_element_type=jnp.float32)
    collapsed_aggregate = first + jnp.einsum(
        "kc,kzxy->czxy", conv_weight, lower_part, preferred_element_type=jnp.float32
    )
    return collapsed_aggregate[:, 1:-1]


def fold_back(gradient, halo_width):
    middle = gradient[..., halo_width : gradient.shape[-1] - halo_width]
    for shift_by in (1, -1):
        if shift_by == 1:
            rim_cells = gradient[..., gradient.shape[-1] - halo_width :]
        else:
            rim_cells = gradient[..., :halo_width]
        arrived = passed_along(rim_cells.astype(jnp.bfloat16), "gy", shift_by).astype(
            rim_cells.dtype
        )
        if shift_by == 1:
            middle = middle.at[..., :halo_width].add(arrived)
        else:
            middle = middle.at[..., middle.shape[-1] - halo_width :].add(arrived)
    result = middle[..., halo_width : middle.shape[-2] - halo_width, :]
    for shift_by in (1, -1):
        if shift_by == 1:
            rim_cells = middle[..., middle.shape[-2] - halo_width :, :]
        else:
            rim_cells = middle[..., :halo_width, :]
        arrived = passed_along(rim_cells.astype(jnp.bfloat16), "gx", shift_by).astype(
            rim_cells.dtype
        )
        if shift_by == 1:
            result = result.at[..., :halo_width, :].add(arrived)
        else:
            result = result.at[..., result.shape[-2] - halo_width :, :].add(arrived)
    return result


def local(features, vessel_label, conv_weight, conv_bias):
    channels, depth_cells, tile_rows, tile_cols = features.shape
    voxels = float(depth_cells * tile_rows * lax.axis_size("gx") * tile_cols * lax.axis_size("gy"))
    skel_reach = ITERS + 2
    cell_neighbourhood = inside_mask(skel_reach, tile_rows, tile_cols)
    fold_width = skel_reach + 1
    joined = jnp.concatenate([features, vessel_label.astype(jnp.bfloat16)[None]], axis=0)
    widened = extend(joined, fold_width)
    padded, logits = convolve(widened[:channels], conv_weight, conv_bias)
    label_cycle = crop_cycle(widened[channels].astype(jnp.float32), 1)
    label_skeleton = skeleton(label_cycle, cell_neighbourhood, skel_reach)

    def local_sums(logit_field):
        prob_cycle = jax.nn.sigmoid(logit_field) * cell_neighbourhood
        return intersection_sums(
            prob_cycle, label_cycle, label_skeleton, cell_neighbourhood, skel_reach
        )

    partial_sums, pullback = jax.vjp(local_sums, logits)

    def backward(cotangents):
        return jnp.stack([pullback(entry)[0] for entry in cotangents])

    totals = lax.psum(jnp.stack(partial_sums), ("gx", "gy"))
    loss_value, slopes = jax.value_and_grad(topology_loss)(totals)
    grad_logits = backward([tuple((slopes[entry] for entry in range(4)))])[0]
    upper_part, lower_part = shifted_stack(grad_logits)
    local_weight = weight_terms(upper_part, lower_part, padded)
    weight_grad, bias_grad = lax.psum((local_weight, jnp.sum(grad_logits)[None]), ("gx", "gy"))
    grad_own = fold_back(feature_terms(upper_part, lower_part, conv_weight), fold_width) * voxels
    return (loss_value, weight_grad, bias_grad, grad_own.astype(jnp.bfloat16))


def solution(mesh):
    in_specs = (P(None, None, "gx", "gy"), P(None, "gx", "gy"), P(), P())
    out_specs = (P(), P(), P(), P(None, None, "gx", "gy"))
    return jax.shard_map(local, mesh=mesh, in_specs=in_specs, out_specs=out_specs, check_vma=False)
```

profile of v0, /device:TPU:1, one launch (start us, length us, event | category | flops | bytes accessed | tf_op | source)
XLA Modules:
  0.0 265.2 jit_solution(332422820204132034)
XLA Ops:
  1.4 1.1 copy_dynamic-update-slice_fusion
  2.5 1.3 collective-permute-start.1
  3.8 5.0 %collective-permute-start = (bf16[33,4,8,128]{3,0,2,1:T(8,128)(2,1)S(1)}, bf16[33,4,8,128]{3,0,2,1:T(8,128)(2,1)S(1)}, u32[]{:S(2)}, u32[]{:S(2)}) collective-permute-start(bf16[33,4,8,128]{3,0,2,1:T(8,128)(2,1)S(1)} %constant_dynamic-update-slice_fusion), channel_id=1, source_target_pairs={{0,8},{8,16},{16,24},{24,32},{32,40},{40,48},{48,56},{56,64},{64,7... | collective-permute-start | bytes 811016 | tf_op jit(solution)/shard_map/ppermute | solution.py:18
  13.7 1.3 copy.71
  15.7 5.3 %collective-permute-start.3 = (bf16[33,4,24,8]{0,3,2,1:T(8,128)(2,1)S(1)}, bf16[33,4,24,8]{0,3,2,1:T(8,128)(2,1)}, u32[]{:S(2)}, u32[]{:S(2)}) collective-permute-start(bf16[33,4,24,8]{0,3,2,1:T(8,128)(2,1)S(1)} %copy.72), channel_id=1, source_target_pairs={{1,0},{2,1},{3,2},{4,3},{5,4},{6,5},{7,6},{9,8},{10,9},{11,10},{12... | collective-permute-start | bytes 152072 | tf_op jit(solution)/shard_map/ppermute | solution.py:19
  21.1 3.0 %collective-permute-start.2 = (bf16[33,4,24,8]{0,3,2,1:T(8,128)(2,1)}, bf16[33,4,24,8]{0,3,2,1:T(8,128)(2,1)S(1)}, u32[]{:S(2)}, u32[]{:S(2)}) collective-permute-start(bf16[33,4,24,8]{0,3,2,1:T(8,128)(2,1)} %copy.71), channel_id=1, source_target_pairs={{0,1},{1,2},{2,3},{3,4},{4,5},{5,6},{6,7},{8,9},{9,10},{10,11},{11... | collective-permute-start | bytes 152072 | tf_op jit(solution)/shard_map/ppermute | solution.py:18
  24.8 2.2 collective-permute-done.2
  27.7 1.6 copy.74
  29.8 1.2 pad_maximum_fusion
  31.0 1.3 copy-done.2
  33.0 2.3 copy.128
  44.0 1.5 multiply_reduce_fusion
  46.3 2.6 pad_maximum_fusion.2
  48.9 83.7 %psum.21 = f32[4]{0:T(128)S(1)} all-reduce(f32[4]{0:T(128)S(1)} %pad_maximum_fusion.2), channel_id=1, replica_groups=mesh['gx'=32,'gy'=8] {'gx','gy'}, use_global_device_ids=true, to_apply=%region_4.6 | all-reduce | flops 4 | bytes 32 | tf_op jit(solution)/shard_map/psum | solution.py:240
  136.9 1.5 divide_multiply_fusion.5
  139.2 1.0 broadcast_multiply_fusion.15
  149.8 1.8 fusion.5
  151.6 5.3 %fusion.379 = (bf16[32,6,24,144]{0,3,2,1:T(8,128)(2,1)S(1)}, f32[32,6,24,144]{0,3,2,1:T(8,128)}) fusion(f32[6,24,144,32]{3,2,1,0:T(8,128)S(1)} %fusion.5, bf16[27,32]{1,0:T(8,128)(2,1)S(1)} %copy-done, bf16[27,6,24,144]{3,2,1,0:T(8,128)(2,1)S(1)} %get-tuple-element.140), kind=kOutput, calls=%fused_computation.833 | convolution fusion | flops 37158912 | bytes 7756992 | tf_op jit(solution)/shard_map/kc,kzxy->czxy/dot_general | solution.py:181
  156.9 2.9 %collective-permute-start.4 = (bf16[32,4,24,8]{0,3,2,1:T(8,128)(2,1)S(1)}, bf16[32,4,24,8]{0,3,2,1:T(8,128)(2,1)S(1)}, u32[]{:S(2)}, u32[]{:S(2)}) collective-permute-start(bf16[32,4,24,8]{0,3,2,1:T(8,128)(2,1)S(1)} %get-tuple-element.213), channel_id=1, source_target_pairs={{0,1},{1,2},{2,3},{3,4},{4,5},{5,6},{6,7},{8,9},{9,10},{10,11},{11... | collective-permute-start | bytes 147464 | tf_op jit(solution)/shard_map/ppermute | solution.py:27
  159.8 1.3 fusion.17
  161.2 2.1 collective-permute-start.5
  163.3 3.2 %slice.1858 = f32[32,4,24,128]{0,3,2,1:T(8,128)S(1)} slice(f32[32,6,24,144]{0,3,2,1:T(8,128)} %get-tuple-element.273), slice={[0:32], [1:5], [0:24], [8:136]} | slice | bytes 3145728 | tf_op jit(solution)/shard_map/slice | solution.py:188
  166.6 1.0 fusion.28
  169.0 1.9 copy-done.1
  170.9 1.1 fusion.368
  172.0 2.4 copy.86
  175.0 1.3 collective-permute-start.7
  176.3 4.3 %collective-permute-start.6 = (bf16[32,4,8,128]{3,2,1,0:T(8,128)(2,1)}, bf16[32,4,8,128]{3,2,1,0:T(8,128)(2,1)S(1)}, u32[]{:S(2)}, u32[]{:S(2)}) collective-permute-start(bf16[32,4,8,128]{3,2,1,0:T(8,128)(2,1)} %copy.86), channel_id=1, source_target_pairs={{0,8},{8,16},{16,24},{24,32},{32,40},{40,48},{48,56},{56,64},{64,7... | collective-permute-start | bytes 786440 | tf_op jit(solution)/shard_map/ppermute | solution.py:27
  180.6 2.7 %fusion.22 = f32[27,32]{1,0:T(8,128)S(1)} fusion(f32[27,32]{1,0:T(8,128)S(1)} %fusion.17, bf16[27,6,24,144]{3,2,1,0:T(8,128)(2,1)S(1)} %get-tuple-element.141, bf16[33,4,24,144]{3,0,2,1:T(8,128)(2,1)} %copy-done.2), kind=kOutput, calls=%fused_computation.19 | convolution fusion | flops 35832672 | bytes 2699520 | tf_op jit(solution)/shard_map/kzxy,czxy->kc/dot_general | solution.py:173
  183.3 76.3 %all-reduce.209 = (f32[27,32]{1,0:T(8,128)}, f32[1]{0:T(128)}) all-reduce(f32[27,32]{1,0:T(8,128)S(1)} %fusion.22, f32[1]{0:T(128)} %bitcast.63), channel_id=1, replica_groups=mesh['gx'=32,'gy'=8] {'gx','gy'}, use_global_device_ids=true, to_apply=%region_5.7 | all-reduce | flops 865 | bytes 6920 | tf_op jit(solution)/shard_map/psum | solution.py:245
  260.6 2.2 fusion.11
  262.8 1.3 copy.90
  (212 shorter events, 31.5 us)
Async XLA Ops:
  0.6 31.7 %copy-start = (bf16[27,32]{1,0:T(8,128)(2,1)S(1)}, bf16[27,32]{1,0:T(8,128)(2,1)}, u32[]{:S(2)}) copy-start(bf16[27,32]{1,0:T(8,128)(2,1)} %param.19) | copy-start | bytes 5188
  2.5 9.9 %collective-permute-start.1 = (bf16[33,4,8,128]{3,0,2,1:T(8,128)(2,1)S(1)}, bf16[33,4,8,128]{3,0,2,1:T(8,128)(2,1)S(1)}, u32[]{:S(2)}, u32[]{:S(2)}) collective-permute-start(bf16[33,4,8,128]{3,0,2,1:T(8,128)(2,1)S(1)} %constant_dynamic-update-slice_fusion), channel_id=1, source_target_pairs={{8,0},{16,8},{24,16},{32,24},{40,32},{48,40},{56,48},{64,56},{72,6... | collective-permute-start | bytes 811016 | tf_op jit(solution)/shard_map/ppermute | solution.py:19
  3.8 9.5 %collective-permute-start = (bf16[33,4,8,128]{3,0,2,1:T(8,128)(2,1)S(1)}, bf16[33,4,8,128]{3,0,2,1:T(8,128)(2,1)S(1)}, u32[]{:S(2)}, u32[]{:S(2)}) collective-permute-start(bf16[33,4,8,128]{3,0,2,1:T(8,128)(2,1)S(1)} %constant_dynamic-update-slice_fusion), channel_id=1, source_target_pairs={{0,8},{8,16},{16,24},{24,32},{32,40},{40,48},{48,56},{56,64},{64,7... | collective-permute-start | bytes 811016 | tf_op jit(solution)/shard_map/ppermute | solution.py:18
  15.7 12.0 %collective-permute-start.3 = (bf16[33,4,24,8]{0,3,2,1:T(8,128)(2,1)S(1)}, bf16[33,4,24,8]{0,3,2,1:T(8,128)(2,1)}, u32[]{:S(2)}, u32[]{:S(2)}) collective-permute-start(bf16[33,4,24,8]{0,3,2,1:T(8,128)(2,1)S(1)} %copy.72), channel_id=1, source_target_pairs={{1,0},{2,1},{3,2},{4,3},{5,4},{6,5},{7,6},{9,8},{10,9},{11,10},{12... | collective-permute-start | bytes 152072 | tf_op jit(solution)/shard_map/ppermute | solution.py:19
  21.1 5.9 %collective-permute-start.2 = (bf16[33,4,24,8]{0,3,2,1:T(8,128)(2,1)}, bf16[33,4,24,8]{0,3,2,1:T(8,128)(2,1)S(1)}, u32[]{:S(2)}, u32[]{:S(2)}) collective-permute-start(bf16[33,4,24,8]{0,3,2,1:T(8,128)(2,1)} %copy.71), channel_id=1, source_target_pairs={{0,1},{1,2},{2,3},{3,4},{4,5},{5,6},{6,7},{8,9},{9,10},{10,11},{11... | collective-permute-start | bytes 152072 | tf_op jit(solution)/shard_map/ppermute | solution.py:18
  31.0 1.3 copy-start.2
  35.8 1.9 copy-start.8
  37.7 1.7 copy-start.7
  44.0 96.3 %copy-start.4 = (f32[4,10,130]{2,1,0:T(8,128)S(1)}, f32[4,10,130]{2,1,0:T(8,128)}, u32[]{:S(2)}) copy-start(f32[4,10,130]{2,1,0:T(8,128)} %get-tuple-element.198) | copy-start | bytes 62404
  45.4 98.8 %copy-start.9 = (f32[16,136]{1,0:T(8,128)S(1)}, f32[16,136]{1,0:T(8,128)}, u32[]{:S(2)}) copy-start(f32[16,136]{1,0:T(8,128)} %get-tuple-element.230) | copy-start | bytes 26116
  138.9 6.1 %copy-start.6 = (f32[18,138]{1,0:T(8,128)S(1)}, f32[18,138]{1,0:T(8,128)}, u32[]{:S(2)}) copy-start(f32[18,138]{1,0:T(8,128)} %get-tuple-element.232) | copy-start | bytes 29812
  140.2 5.2 %copy-start.5 = (f32[20,140]{1,0:T(8,128)S(1)}, f32[20,140]{1,0:T(8,128)}, u32[]{:S(2)}) copy-start(f32[20,140]{1,0:T(8,128)} %get-tuple-element.234) | copy-start | bytes 33604
  141.3 4.5 %copy-start.10 = (f32[4,8,128]{2,1,0:T(8,128)S(1)}, f32[4,8,128]{2,1,0:T(8,128)}, u32[]{:S(2)}) copy-start(f32[4,8,128]{2,1,0:T(8,128)} %get-tuple-element.209) | copy-start | bytes 49156
  151.6 8.2 %copy-start.3 = (bf16[33,4,24,144]{3,0,2,1:T(8,128)(2,1)S(1)}, bf16[33,4,24,144]{3,0,2,1:T(8,128)(2,1)}, u32[]{:S(2)}) copy-start(bf16[33,4,24,144]{3,0,2,1:T(8,128)(2,1)} %copy-done.2) | copy-start | bytes 2737156
  156.9 9.6 %collective-permute-start.4 = (bf16[32,4,24,8]{0,3,2,1:T(8,128)(2,1)S(1)}, bf16[32,4,24,8]{0,3,2,1:T(8,128)(2,1)S(1)}, u32[]{:S(2)}, u32[]{:S(2)}) collective-permute-start(bf16[32,4,24,8]{0,3,2,1:T(8,128)(2,1)S(1)} %get-tuple-element.213), channel_id=1, source_target_pairs={{0,1},{1,2},{2,3},{3,4},{4,5},{5,6},{6,7},{8,9},{9,10},{10,11},{11... | collective-permute-start | bytes 147464 | tf_op jit(solution)/shard_map/ppermute | solution.py:27
  161.2 7.0 %collective-permute-start.5 = (bf16[32,4,24,8]{0,3,2,1:T(8,128)(2,1)S(1)}, bf16[32,4,24,8]{0,3,2,1:T(8,128)(2,1)S(1)}, u32[]{:S(2)}, u32[]{:S(2)}) collective-permute-start(bf16[32,4,24,8]{0,3,2,1:T(8,128)(2,1)S(1)} %get-tuple-element.212), channel_id=1, source_target_pairs={{1,0},{2,1},{3,2},{4,3},{5,4},{6,5},{7,6},{9,8},{10,9},{11,10},{12... | collective-permute-start | bytes 147464 | tf_op jit(solution)/shard_map/ppermute | solution.py:27
  168.3 2.6 copy-start.1
  175.0 85.1 %collective-permute-start.7 = (bf16[32,4,8,128]{3,2,1,0:T(8,128)(2,1)S(1)}, bf16[32,4,8,128]{3,2,1,0:T(8,128)(2,1)S(1)}, u32[]{:S(2)}, u32[]{:S(2)}) collective-permute-start(bf16[32,4,8,128]{3,2,1,0:T(8,128)(2,1)S(1)} %copy.88), channel_id=1, source_target_pairs={{8,0},{16,8},{24,16},{32,24},{40,32},{48,40},{56,48},{64,56},{72,6... | collective-permute-start | bytes 786440 | tf_op jit(solution)/shard_map/ppermute | solution.py:27
  176.3 83.3 %collective-permute-start.6 = (bf16[32,4,8,128]{3,2,1,0:T(8,128)(2,1)}, bf16[32,4,8,128]{3,2,1,0:T(8,128)(2,1)S(1)}, u32[]{:S(2)}, u32[]{:S(2)}) collective-permute-start(bf16[32,4,8,128]{3,2,1,0:T(8,128)(2,1)} %copy.86), channel_id=1, source_target_pairs={{0,8},{8,16},{16,24},{24,32},{32,40},{40,48},{48,56},{56,64},{64,7... | collective-permute-start | bytes 786440 | tf_op jit(solution)/shard_map/ppermute | solution.py:27
where the time goes:
time: 266 us; the launch traced here: 265 us
  blocking collectives  160 us (60%)
  other arithmetic  33 us (12%)
  starting transfers between devices  25.3 us (10%)
  local copies, waits for them, and re-layouts  24.9 us (9%)
  matrix products  11.7 us (4%)
  between operations  6.76 us (3%)
  waiting for transfers between devices  3.59 us (1%)
    psum x1, blocking collectives, local(): totals = lax.psum(jnp.stack(partial_sums), ('gx', 'gy'))  83.7 us
    psum x1, blocking collectives, local(): lax.psum((local_weight, jnp.sum(grad_logits)[None]), ('gx', 'gy'))  76.3 us
    ppermute x4, starting transfers between devices, passed_along(): lax.ppermute(value, axis, [(source, source + steps) for source in range(i...  10.6 us
    ppermute x2, starting transfers between devices, padded_2(): before = lax.ppermute(last, axis, up)  8.04 us
    unnamed x51, local copies, waits for them, and re-layouts  7.28 us
    ppermute x2, starting transfers between devices, padded_2(): after = lax.ppermute(initial, axis, down)  6.62 us
    mul x11, other arithmetic, soft_erode(): -softmin_sharpness * jnp.log(middle_cell / 3.0 + neighbouring_cells / 9.0)  5.88 us
  transfers between devices with their start and end apart: 8, of which 3 were waited for; matrix products, arithmetic and copies ran while one was open for 5% of the time, Pallas kernels for 0%

commit v1 on v0

--- a/solution.py
+++ b/solution.py
@@ -237,7 +237,8 @@
     def backward(cotangents):
         return jnp.stack([pullback(entry)[0] for entry in cotangents])
 
-    totals = lax.psum(jnp.stack(partial_sums), ("gx", "gy"))
+    half = lax.psum(jnp.stack(partial_sums), "gy")
+    totals = lax.psum(half, "gx")
     loss_value, slopes = jax.value_and_grad(topology_loss)(totals)
     grad_logits = backward([tuple((slopes[entry] for entry in range(4)))])[0]
     upper_part, lower_part = shifted_stack(grad_logits)

time: 266 us -> 271 us (1.019)
  starting transfers between devices: 25.3 us -> 38.2 us
  blocking collectives: 160 us -> 152 us
    ppermute x4, starting transfers between devices: 10.6 us -> 23.5 us  [passed_along(): lax.ppermute(value, axis, [(source, source + steps) for source in range(i...]
    psum x1 -> x2, blocking collectives: 83.7 us -> 78.1 us  [the longest x1 65.2 us: local(): totals = lax.psum(half, 'gx')]
where the time goes in v1:
time: 271 us; the launch traced here: 270 us
  blocking collectives  152 us (56%)
  starting transfers between devices  38.2 us (14%)
  other arithmetic  33 us (12%)
  local copies, waits for them, and re-layouts  24.9 us (9%)
  matrix products  11.7 us (4%)
  between operations  6.8 us (3%)
  waiting for transfers between devices  3.29 us (1%)
    psum x1, blocking collectives, local(): lax.psum((local_weight, jnp.sum(grad_logits)[None]), ('gx', 'gy'))  74 us
    psum x1, blocking collectives, local(): totals = lax.psum(half, 'gx')  65.2 us
    ppermute x4, starting transfers between devices, passed_along(): lax.ppermute(value, axis, [(source, source + steps) for source in range(i...  23.5 us
    psum x1, blocking collectives, local(): half = lax.psum(jnp.stack(partial_sums), 'gy')  13 us
    ppermute x2, starting transfers between devices, padded_2(): before = lax.ppermute(last, axis, up)  8.04 us
    unnamed x51, local copies, waits for them, and re-layouts  7.24 us
    ppermute x2, starting transfers between devices, padded_2(): after = lax.ppermute(initial, axis, down)  6.62 us
    mul x11, other arithmetic, soft_erode(): -softmin_sharpness * jnp.log(middle_cell / 3.0 + neighbouring_cells / 9.0)  5.84 us
  transfers between devices with their start and end apart: 8, of which 3 were waited for; matrix products, arithmetic and copies ran while one was open for 5% of the time, Pallas kernels for 0%

profile of v1, /device:TPU:1, one launch (start us, length us, event | category | flops | bytes accessed | tf_op | source)
XLA Modules:
  0.0 269.9 jit_solution(8864720336116154564)
XLA Ops:
  1.4 1.1 copy_dynamic-update-slice_fusion
  2.5 1.3 collective-permute-start.1
  3.8 5.0 %collective-permute-start = (bf16[33,4,8,128]{3,0,2,1:T(8,128)(2,1)S(1)}, bf16[33,4,8,128]{3,0,2,1:T(8,128)(2,1)S(1)}, u32[]{:S(2)}, u32[]{:S(2)}) collective-permute-start(bf16[33,4,8,128]{3,0,2,1:T(8,128)(2,1)S(1)} %constant_dynamic-update-slice_fusion), channel_id=1, source_target_pairs={{0,8},{8,16},{16,24},{24,32},{32,40},{40,48},{48,56},{56,64},{64,7... | collective-permute-start | bytes 811016 | tf_op jit(solution)/shard_map/ppermute | solution.py:18
  13.7 1.3 copy.71
  15.7 5.3 %collective-permute-start.3 = (bf16[33,4,24,8]{0,3,2,1:T(8,128)(2,1)S(1)}, bf16[33,4,24,8]{0,3,2,1:T(8,128)(2,1)}, u32[]{:S(2)}, u32[]{:S(2)}) collective-permute-start(bf16[33,4,24,8]{0,3,2,1:T(8,128)(2,1)S(1)} %copy.72), channel_id=1, source_target_pairs={{1,0},{2,1},{3,2},{4,3},{5,4},{6,5},{7,6},{9,8},{10,9},{11,10},{12... | collective-permute-start | bytes 152072 | tf_op jit(solution)/shard_map/ppermute | solution.py:19
  21.1 3.0 %collective-permute-start.2 = (bf16[33,4,24,8]{0,3,2,1:T(8,128)(2,1)}, bf16[33,4,24,8]{0,3,2,1:T(8,128)(2,1)S(1)}, u32[]{:S(2)}, u32[]{:S(2)}) collective-permute-start(bf16[33,4,24,8]{0,3,2,1:T(8,128)(2,1)} %copy.71), channel_id=1, source_target_pairs={{0,1},{1,2},{2,3},{3,4},{4,5},{5,6},{6,7},{8,9},{9,10},{10,11},{11... | collective-permute-start | bytes 152072 | tf_op jit(solution)/shard_map/ppermute | solution.py:18
  24.8 2.2 collective-permute-done.2
  27.7 1.6 copy.74
  29.8 1.2 pad_maximum_fusion
  31.0 1.3 copy-done.2
  32.9 2.3 copy.128
  43.9 1.5 multiply_reduce_fusion
  46.3 2.7 pad_maximum_fusion.2
  48.9 13.0 %psum.28 = f32[4]{0:T(128)S(1)} all-reduce(f32[4]{0:T(128)S(1)} %pad_maximum_fusion.2), channel_id=1, replica_groups=mesh['gx'=32,'gy'=8] {'gy'}, use_global_device_ids=true, to_apply=%region_4.6 | all-reduce | flops 4 | bytes 32 | tf_op jit(solution)/shard_map/psum | solution.py:240
  61.9 65.2 %psum.29 = f32[4]{0:T(128)S(1)} all-reduce(f32[4]{0:T(128)S(1)} %psum.28), channel_id=1, replica_groups=mesh['gx'=32,'gy'=8] {'gx'}, use_global_device_ids=true, to_apply=%region_5.7 | all-reduce | flops 4 | bytes 32 | tf_op jit(solution)/shard_map/psum | solution.py:241
  131.4 1.5 divide_multiply_fusion.5
  144.4 1.8 fusion.5
  146.2 5.3 %fusion.379 = (bf16[32,6,24,144]{0,3,2,1:T(8,128)(2,1)S(1)}, f32[32,6,24,144]{0,3,2,1:T(8,128)}) fusion(f32[6,24,144,32]{3,2,1,0:T(8,128)S(1)} %fusion.5, bf16[27,32]{1,0:T(8,128)(2,1)S(1)} %copy-done, bf16[27,6,24,144]{3,2,1,0:T(8,128)(2,1)S(1)} %get-tuple-element.140), kind=kOutput, calls=%fused_computation.833 | convolution fusion | flops 37158912 | bytes 7756992 | tf_op jit(solution)/shard_map/kc,kzxy->czxy/dot_general | solution.py:181
  151.5 15.5 %collective-permute-start.4 = (bf16[32,4,24,8]{0,3,2,1:T(8,128)(2,1)S(1)}, bf16[32,4,24,8]{0,3,2,1:T(8,128)(2,1)S(1)}, u32[]{:S(2)}, u32[]{:S(2)}) collective-permute-start(bf16[32,4,24,8]{0,3,2,1:T(8,128)(2,1)S(1)} %get-tuple-element.213), channel_id=1, source_target_pairs={{0,1},{1,2},{2,3},{3,4},{4,5},{5,6},{6,7},{8,9},{9,10},{10,11},{11... | collective-permute-start | bytes 147464 | tf_op jit(solution)/shard_map/ppermute | solution.py:27
  167.0 1.3 fusion.17
  168.4 2.5 collective-permute-start.5
  170.9 3.2 %slice.1858 = f32[32,4,24,128]{0,3,2,1:T(8,128)S(1)} slice(f32[32,6,24,144]{0,3,2,1:T(8,128)} %get-tuple-element.273), slice={[0:32], [1:5], [0:24], [8:136]} | slice | bytes 3145728 | tf_op jit(solution)/shard_map/slice | solution.py:188
  174.1 1.0 fusion.28
  176.2 1.9 copy-done.1
  178.1 1.1 fusion.368
  179.2 2.4 copy.86
  182.1 1.3 collective-permute-start.7
  183.4 4.2 %collective-permute-start.6 = (bf16[32,4,8,128]{3,2,1,0:T(8,128)(2,1)}, bf16[32,4,8,128]{3,2,1,0:T(8,128)(2,1)S(1)}, u32[]{:S(2)}, u32[]{:S(2)}) collective-permute-start(bf16[32,4,8,128]{3,2,1,0:T(8,128)(2,1)} %copy.86), channel_id=1, source_target_pairs={{0,8},{8,16},{16,24},{24,32},{32,40},{40,48},{48,56},{56,64},{64,7... | collective-permute-start | bytes 786440 | tf_op jit(solution)/shard_map/ppermute | solution.py:27
  187.7 2.7 fusion.22
  190.4 74.0 %all-reduce.209 = (f32[27,32]{1,0:T(8,128)}, f32[1]{0:T(128)}) all-reduce(f32[27,32]{1,0:T(8,128)S(1)} %fusion.22, f32[1]{0:T(128)} %bitcast.63), channel_id=1, replica_groups=mesh['gx'=32,'gy'=8] {'gx','gy'}, use_global_device_ids=true, to_apply=%region_6.8 | all-reduce | flops 865 | bytes 6920 | tf_op jit(solution)/shard_map/psum | solution.py:246
  265.4 2.2 fusion.11
  267.6 1.3 copy.90
  (213 shorter events, 32.2 us)
Async XLA Ops:
  0.6 31.7 %copy-start = (bf16[27,32]{1,0:T(8,128)(2,1)S(1)}, bf16[27,32]{1,0:T(8,128)(2,1)}, u32[]{:S(2)}) copy-start(bf16[27,32]{1,0:T(8,128)(2,1)} %param.19) | copy-start | bytes 5188
  2.5 9.9 %collective-permute-start.1 = (bf16[33,4,8,128]{3,0,2,1:T(8,128)(2,1)S(1)}, bf16[33,4,8,128]{3,0,2,1:T(8,128)(2,1)S(1)}, u32[]{:S(2)}, u32[]{:S(2)}) collective-permute-start(bf16[33,4,8,128]{3,0,2,1:T(8,128)(2,1)S(1)} %constant_dynamic-update-slice_fusion), channel_id=1, source_target_pairs={{8,0},{16,8},{24,16},{32,24},{40,32},{48,40},{56,48},{64,56},{72,6... | collective-permute-start | bytes 811016 | tf_op jit(solution)/shard_map/ppermute | solution.py:19
  3.8 9.5 %collective-permute-start = (bf16[33,4,8,128]{3,0,2,1:T(8,128)(2,1)S(1)}, bf16[33,4,8,128]{3,0,2,1:T(8,128)(2,1)S(1)}, u32[]{:S(2)}, u32[]{:S(2)}) collective-permute-start(bf16[33,4,8,128]{3,0,2,1:T(8,128)(2,1)S(1)} %constant_dynamic-update-slice_fusion), channel_id=1, source_target_pairs={{0,8},{8,16},{16,24},{24,32},{32,40},{40,48},{48,56},{56,64},{64,7... | collective-permute-start | bytes 811016 | tf_op jit(solution)/shard_map/ppermute | solution.py:18
  15.7 12.0 %collective-permute-start.3 = (bf16[33,4,24,8]{0,3,2,1:T(8,128)(2,1)S(1)}, bf16[33,4,24,8]{0,3,2,1:T(8,128)(2,1)}, u32[]{:S(2)}, u32[]{:S(2)}) collective-permute-start(bf16[33,4,24,8]{0,3,2,1:T(8,128)(2,1)S(1)} %copy.72), channel_id=1, source_target_pairs={{1,0},{2,1},{3,2},{4,3},{5,4},{6,5},{7,6},{9,8},{10,9},{11,10},{12... | collective-permute-start | bytes 152072 | tf_op jit(solution)/shard_map/ppermute | solution.py:19
  21.1 5.9 %collective-permute-start.2 = (bf16[33,4,24,8]{0,3,2,1:T(8,128)(2,1)}, bf16[33,4,24,8]{0,3,2,1:T(8,128)(2,1)S(1)}, u32[]{:S(2)}, u32[]{:S(2)}) collective-permute-start(bf16[33,4,24,8]{0,3,2,1:T(8,128)(2,1)} %copy.71), channel_id=1, source_target_pairs={{0,1},{1,2},{2,3},{3,4},{4,5},{5,6},{6,7},{8,9},{9,10},{10,11},{11... | collective-permute-start | bytes 152072 | tf_op jit(solution)/shard_map/ppermute | solution.py:18
  31.0 1.3 copy-start.2
  35.8 1.9 copy-start.8
  37.7 1.7 copy-start.7
  43.9 91.0 %copy-start.4 = (f32[4,10,130]{2,1,0:T(8,128)S(1)}, f32[4,10,130]{2,1,0:T(8,128)}, u32[]{:S(2)}) copy-start(f32[4,10,130]{2,1,0:T(8,128)} %get-tuple-element.198) | copy-start | bytes 62404
  45.4 93.4 %copy-start.9 = (f32[16,136]{1,0:T(8,128)S(1)}, f32[16,136]{1,0:T(8,128)}, u32[]{:S(2)}) copy-start(f32[16,136]{1,0:T(8,128)} %get-tuple-element.230) | copy-start | bytes 26116
  133.4 6.1 %copy-start.6 = (f32[18,138]{1,0:T(8,128)S(1)}, f32[18,138]{1,0:T(8,128)}, u32[]{:S(2)}) copy-start(f32[18,138]{1,0:T(8,128)} %get-tuple-element.232) | copy-start | bytes 29812
  134.7 5.2 %copy-start.5 = (f32[20,140]{1,0:T(8,128)S(1)}, f32[20,140]{1,0:T(8,128)}, u32[]{:S(2)}) copy-start(f32[20,140]{1,0:T(8,128)} %get-tuple-element.234) | copy-start | bytes 33604
  135.8 4.5 %copy-start.10 = (f32[4,8,128]{2,1,0:T(8,128)S(1)}, f32[4,8,128]{2,1,0:T(8,128)}, u32[]{:S(2)}) copy-start(f32[4,8,128]{2,1,0:T(8,128)} %get-tuple-element.209) | copy-start | bytes 49156
  146.2 20.9 %copy-start.3 = (bf16[33,4,24,144]{3,0,2,1:T(8,128)(2,1)S(1)}, bf16[33,4,24,144]{3,0,2,1:T(8,128)(2,1)}, u32[]{:S(2)}) copy-start(bf16[33,4,24,144]{3,0,2,1:T(8,128)(2,1)} %copy-done.2) | copy-start | bytes 2737156
  151.5 22.6 %collective-permute-start.4 = (bf16[32,4,24,8]{0,3,2,1:T(8,128)(2,1)S(1)}, bf16[32,4,24,8]{0,3,2,1:T(8,128)(2,1)S(1)}, u32[]{:S(2)}, u32[]{:S(2)}) collective-permute-start(bf16[32,4,24,8]{0,3,2,1:T(8,128)(2,1)S(1)} %get-tuple-element.213), channel_id=1, source_target_pairs={{0,1},{1,2},{2,3},{3,4},{4,5},{5,6},{6,7},{8,9},{9,10},{10,11},{11... | collective-permute-start | bytes 147464 | tf_op jit(solution)/shard_map/ppermute | solution.py:27
  168.4 7.0 %collective-permute-start.5 = (bf16[32,4,24,8]{0,3,2,1:T(8,128)(2,1)S(1)}, bf16[32,4,24,8]{0,3,2,1:T(8,128)(2,1)S(1)}, u32[]{:S(2)}, u32[]{:S(2)}) collective-permute-start(bf16[32,4,24,8]{0,3,2,1:T(8,128)(2,1)S(1)} %get-tuple-element.212), channel_id=1, source_target_pairs={{1,0},{2,1},{3,2},{4,3},{5,4},{6,5},{7,6},{9,8},{10,9},{11,10},{12... | collective-permute-start | bytes 147464 | tf_op jit(solution)/shard_map/ppermute | solution.py:27
  175.5 2.6 copy-start.1
  182.1 82.7 %collective-permute-start.7 = (bf16[32,4,8,128]{3,2,1,0:T(8,128)(2,1)S(1)}, bf16[32,4,8,128]{3,2,1,0:T(8,128)(2,1)S(1)}, u32[]{:S(2)}, u32[]{:S(2)}) collective-permute-start(bf16[32,4,8,128]{3,2,1,0:T(8,128)(2,1)S(1)} %copy.88), channel_id=1, source_target_pairs={{8,0},{16,8},{24,16},{32,24},{40,32},{48,40},{56,48},{64,56},{72,6... | collective-permute-start | bytes 786440 | tf_op jit(solution)/shard_map/ppermute | solution.py:27
  183.4 80.9 %collective-permute-start.6 = (bf16[32,4,8,128]{3,2,1,0:T(8,128)(2,1)}, bf16[32,4,8,128]{3,2,1,0:T(8,128)(2,1)S(1)}, u32[]{:S(2)}, u32[]{:S(2)}) collective-permute-start(bf16[32,4,8,128]{3,2,1,0:T(8,128)(2,1)} %copy.86), channel_id=1, source_target_pairs={{0,8},{8,16},{16,24},{24,32},{32,40},{40,48},{48,56},{56,64},{64,7... | collective-permute-start | bytes 786440 | tf_op jit(solution)/shard_map/ppermute | solution.py:27
